TPU v7x, 32 devices: a whole 2x2x4 slice. The times are simulated.
32 devices in a mesh: rep: 2 (over y), fsdp: 16 (over z, x, core).
Axes of the slice: x: 2, y: 2, z: 4, core: 2. Of those that a mesh axis runs over, the one named last changes fastest.
Arguments:
- hidden: bfloat16 [8192, 5120], P(('rep', 'fsdp')), may hold values from -6 to 6
- weight: bfloat16 [640, 64, 128], P('fsdp'), may hold values from -0.078125 to 0.078125
- momentum: float32 [2, 640, 64, 128], P('rep', 'fsdp'), may hold values from -6 to 6
- gradient: bfloat16 [2, 640, 64, 128], P('rep', 'fsdp'), may hold values from -6 to 6
- indices: int32 [2, 1280, 32], P('rep', 'fsdp'), may hold values from 0 to 4095, as said below
- counts: int32 [2, 1280], P('rep', 'fsdp'), may hold values from 1 to 32, as said below
Outputs:
- key_states: bfloat16 [8192, 1024], P(('rep', 'fsdp'))
- update: bfloat16 [640, 64, 128], P('fsdp', 'rep')
- new_momentum: float32 [2, 640, 64, 128], P('rep', 'fsdp')
Inputs may be any that keep to these rules, and one draw needn't show every extreme that they name: `indices`: the 32 numbers of one replica's block differ from one another. `counts`: some block of every replica keeps all 32.
All inputs are finite; a program needn't handle non-finite values.
Results may differ from a plain program's by a relative error of at most 0.0095.
Values may be sent and summed in bfloat16 or wider, within the bound.
A program may use at most 128 MiB of HBM per device.

v0:
```python
import functools

import jax
import jax.numpy as jnp
import numpy as np
from jax import lax
from jax.experimental import pallas as pl
from jax.experimental.pallas import tpu as pltpu
from jax.sharding import PartitionSpec as P

decay_rate = 0.999
step_size = 0.01
tiny_eps = 1e-06
exact = lax.Precision.HIGHEST
MESH = pl.DeviceIdType.MESH
CHUNKS = 5


def cosine_table(length):
    wave = np.arange(length, dtype=np.float64)[:, None]
    place = np.arange(length, dtype=np.float64)[None, :]
    table = np.cos(np.pi * (2.0 * place + 1.0) * wave / (2.0 * length)) * np.sqrt(2.0 / length)
    return np.where(wave == 0.0, table * np.sqrt(0.5), table)


def split(value):
    high = value.astype(jnp.bfloat16)
    return high, (value - high.astype(jnp.float32)).astype(jnp.bfloat16)


def dot(a, b):
    return jnp.dot(a, b, preferred_element_type=jnp.float32)


def dot_nt(a, b):
    return lax.dot_general(a, b, (((1,), (1,)), ((), ())), preferred_element_type=jnp.float32)


def right3(a, b_high, b_low):
    high, low = split(a)
    return dot(high, b_high) + (dot(high, b_low) + dot(low, b_high))


def left3(a_high, a_low, b):
    high, low = split(b)
    return dot(a_high, high) + (dot(a_high, low) + dot(a_low, high))


def fused_kernel(
    hidden,
    weight,
    momentum,
    gradient,
    index,
    basis,
    basis_high,
    basis_low,
    keys,
    update,
    new_momentum,
    blocks,
    tokens,
    total,
    partial,
    spectra,
    kept,
    kept_other,
    index_other,
    recv_sem,
    z_sem,
    x_sem,
    y_sem,
    small_send,
    small_recv,
    part_send,
    part_recv,
):
    tiles, side, cols = weight.shape
    per = tiles // CHUNKS
    rows = per * side
    half = tiles * side
    own_tokens = hidden.shape[0]
    pair = 2 * side
    four = 4 * side

    r = lax.axis_index("rep")
    f = lax.axis_index("fsdp")
    z, x, c = f // 4, (f // 2) % 2, f % 2
    middle = jnp.logical_and(z > 0, z < 3)
    up_ok, down_ok = z < 3, z > 0
    y_dev = (1 - r, f)
    x_dev = (r, z * 4 + (1 - x) * 2 + c)
    sib_dev = (r, z * 4 + x * 2 + (1 - c))
    up_dev = (r, jnp.minimum(f + 4, 15 - 3 + f % 4))
    down_dev = (r, jnp.maximum(f - 4, f % 4))

    barrier = pltpu.get_barrier_semaphore()
    for device in (y_dev, x_dev, sib_dev):
        pl.semaphore_signal(barrier, inc=1, device_id=device, device_id_type=MESH)

    @pl.when(up_ok)
    def _():
        pl.semaphore_signal(barrier, inc=1, device_id=up_dev, device_id_type=MESH)

    @pl.when(down_ok)
    def _():
        pl.semaphore_signal(barrier, inc=1, device_id=down_dev, device_id_type=MESH)

    pl.semaphore_wait(barrier, jnp.where(middle, 5, 4))

    def remote(src, dst, send, recv, device):
        return pltpu.make_async_remote_copy(
            src_ref=src, dst_ref=dst, send_sem=send, recv_sem=recv, device_id=device, device_id_type=MESH
        )

    index_copy = remote(index, index_other, small_send.at[0], small_recv.at[0], y_dev)
    index_copy.start()
    token_copy = remote(
        hidden.at[:, pl.ds(pl.multiple_of((1 - c) * half, 128), half)],
        tokens.at[pl.ds(own_tokens, own_tokens)],
        small_send.at[1],
        small_recv.at[1],
        sib_dev,
    )
    token_copy.start()
    token_local = pltpu.make_async_copy(
        hidden.at[:, pl.ds(pl.multiple_of(c * half, 128), half)],
        tokens.at[pl.ds(0, own_tokens)],
        small_send.at[3],
    )
    token_local.start()

    def place(p):
        return jnp.where(r == 0, p, CHUNKS - 1 - p)

    def layer(j):
        if j == 0:
            return z
        at_end = jnp.where(z == 0, j, 3 - j)
        flip = (1, 3, 2)[j - 1]
        bits = z // 2, z % 2
        inner = ((bits[0] + flip // 2) % 2) * 2 + (bits[1] + flip % 2) % 2
        return jnp.where(middle, inner, at_end)

    def chunk(o, p):
        q = place(p)
        ref = blocks.at[o, pl.ds(pl.multiple_of(q * rows, rows), rows)]
        return ref, o * CHUNKS + q

    def move(o, p, sems, device):
        ref, n = chunk(o, p)
        return remote(ref, ref, sems.at[n], recv_sem.at[n], device)

    def z_move(o, p, way):
        return move(o, p, z_sem.at[way], up_dev if way == 0 else down_dev)

    lane = lax.broadcasted_iota(jnp.int32, (1, cols), 1)
    row_iota = lax.broadcasted_iota(jnp.int32, (side, cols), 0)
    col_iota = lax.broadcasted_iota(jnp.int32, (cols, cols), 0)
    left_lanes = lane < side
    second = jnp.where(lane % side >= side // 2, side, 0)

    def hot_rows(idx):
        return row_iota == (idx >> 6)

    def hot_cols(idx):
        return (col_iota == ((idx & (side - 1)) + second)).astype(jnp.bfloat16)

    def both_halves(value):
        return jnp.concatenate([value[:four], value[four:]], axis=1)

    def stacked(value):
        return jnp.concatenate([value[:, :cols], value[:, cols:]], axis=0)

    def inverse(coefficients):
        part = right3(coefficients, basis_high[0, :pair, :pair], basis_low[0, :pair, :pair])
        return stacked(left3(basis_high[1], basis_low[1], both_halves(part)))

    def tile_slice(q):
        return pl.ds(pl.multiple_of(q * per, per), per)

    def forward(q, carry):
        here = tile_slice(q)
        moment = decay_rate * momentum[0, here] + gradient[0, here].astype(jnp.float32)
        new_momentum[0, here] = moment
        part = jnp.dot(
            moment.reshape(rows, cols),
            basis[1, :pair, :pair],
            precision=exact,
            preferred_element_type=jnp.float32,
        )
        spectrum = stacked(
            jnp.dot(basis[0], both_halves(part), precision=exact, preferred_element_type=jnp.float32)
        )
        spectra[pl.ds(pl.multiple_of(q * rows, rows), rows)] = spectrum
        idx = index[here]
        found = []
        for t in range(per):
            one = idx[t : t + 1]
            high, low = split(spectrum[t * side : (t + 1) * side])
            taken = dot(jnp.concatenate([high, low], axis=0), hot_cols(one))
            taken = taken[:side] + taken[side:]
            found.append(jnp.sum(jnp.where(hot_rows(one), taken, 0.0), axis=0, keepdims=True))
        kept[here] = jnp.concatenate(found, axis=0)
        return carry

    lax.fori_loop(0, CHUNKS, forward, 0)
    kept_copy = remote(kept, kept_other, small_send.at[2], small_recv.at[2], y_dev)
    kept_copy.start()
    index_copy.wait_recv()
    kept_copy.wait_recv()

    own_block = 2 * z + x

    def step(p, carry):
        q = place(p)
        here = tile_slice(q)
        idx = jnp.where(left_lanes, index[here], index_other[here])
        values = jnp.where(left_lanes, kept[here], kept_other[here]) * 0.5
        dense = []
        for t in range(per):
            one = idx[t : t + 1]
            high, low = split(jnp.where(hot_rows(one), values[t : t + 1], 0.0))
            put = dot_nt(jnp.concatenate([high, low], axis=0), hot_cols(one))
            tile = put[:side] + put[side:]
            energy = jnp.sum(tile * tile, axis=0, keepdims=True)
            left = jnp.sum(jnp.where(left_lanes, energy, 0.0), axis=1, keepdims=True)
            right = jnp.sum(jnp.where(left_lanes, 0.0, energy), axis=1, keepdims=True)
            energy = jnp.where(left_lanes, left, right)
            dense.append(tile * lax.rsqrt(energy / (side * side) + tiny_eps))
        raw = inverse(jnp.concatenate(dense, axis=0))
        direction = jnp.tanh(raw).astype(jnp.bfloat16).astype(jnp.float32)
        tiled = direction.reshape(per, side, cols)
        shown = jnp.where(r == 0, tiled[:, : side // 2], tiled[:, side // 2 :])
        update[here] = shown.astype(jnp.bfloat16)
        old = weight[here].astype(jnp.float32).reshape(rows, cols)
        blocks[own_block, pl.ds(pl.multiple_of(q * rows, rows), rows)] = (
            old - step_size * direction
        ).astype(jnp.bfloat16)

        @pl.when(jnp.logical_and(up_ok, p < 4))
        def _():
            z_move(own_block, p, 0).start()

        @pl.when(jnp.logical_and(down_ok, p < 4))
        def _():
            z_move(own_block, p, 1).start()

        @pl.when(p < 3)
        def _():
            move(own_block, p, x_sem, x_dev).start()

        return carry

    lax.fori_loop(0, CHUNKS, step, 0)

    def settle(q, carry):
        here = tile_slice(q)
        idx = index[here]
        spectrum = spectra[pl.ds(pl.multiple_of(q * rows, rows), rows)]
        masks = []
        for t in range(per):
            one = idx[t : t + 1]
            hot = jnp.where(jnp.logical_and(hot_rows(one), left_lanes), 1.0, 0.0).astype(jnp.bfloat16)
            masks.append(dot_nt(hot, hot_cols(one)))
        own = jnp.where(jnp.concatenate(masks, axis=0) > 0.5, spectrum, 0.0)
        new_momentum[0, here] = new_momentum[0, here] - inverse(own).reshape(per, side, cols)
        return carry

    lax.fori_loop(0, CHUNKS, settle, 0)
    token_local.wait()
    token_copy.wait_recv()

    def arrived(o, p):
        move(o, p, x_sem, x_dev).wait_recv()

    def from_z(j, p):
        o = 2 * layer(j) + x
        arrived(o, p)
        below = layer(j) < z

        @pl.when(jnp.logical_and(below, up_ok))
        def _():
            z_move(o, p, 0).start()

        @pl.when(jnp.logical_and(jnp.logical_not(below), down_ok))
        def _():
            z_move(o, p, 1).start()

        if p < 3:
            move(o, p, x_sem, x_dev).start()
        if p == 0:
            move(o, p, y_sem, y_dev).start()

    def from_x(j, p):
        o = 2 * layer(j) + (1 - x)
        arrived(o, p)
        if p < 2:
            move(o, p, y_sem, y_dev).start()

    def part_copy(j):
        return remote(
            total.at[j, pl.ds(own_tokens, own_tokens)], partial.at[j], part_send.at[j], part_recv.at[j], sib_dev
        )

    def multiply(j):
        o = 2 * layer(j)

        def product(k):
            deep = pl.ds(pl.multiple_of(k * rows, rows), rows)
            both = jnp.concatenate([blocks[o, deep], blocks[o + 1, deep]], axis=1)
            return dot(tokens[:, deep], both)

        total[j] = product(0)

        def add(k, carry):
            total[j] += product(k)
            return carry

        lax.fori_loop(1, CHUNKS, add, 0)
        part_copy(j).start()

    for j in range(5):
        for p in range(4):
            if 1 <= j + 1 <= 3:
                from_z(j + 1, p)
            if j < 4 and p < 3:
                from_x(j, p)
        if j < 4:
            if j > 0:
                arrived(2 * layer(j) + x, 4)
            arrived(2 * layer(j) + (1 - x), 4)
            arrived(2 * layer(j) + (1 - x), 3)
            multiply(j)

    for j in range(4):
        part_copy(j).wait_recv()
        columns = pl.ds(pl.multiple_of(layer(j) * 2 * cols, 2 * cols), 2 * cols)
        keys[:, columns] = (total[j, :own_tokens] + partial[j]).astype(jnp.bfloat16)

    index_copy.wait_send()
    token_copy.wait_send()
    kept_copy.wait_send()
    for j in range(4):
        part_copy(j).wait_send()
        o = 2 * layer(j) + x
        below = layer(j) < z
        above = layer(j) > z
        goes_up = jnp.logical_and(jnp.logical_not(above), up_ok)
        goes_down = jnp.logical_and(jnp.logical_not(below), down_ok)
        for p in range(4):

            @pl.when(goes_up)
            def _():
                z_move(o, p, 0).wait_send()

            @pl.when(goes_down)
            def _():
                z_move(o, p, 1).wait_send()

            if p < 3:
                move(o, p, x_sem, x_dev).wait_send()
        if j > 0:
            move(o, 0, y_sem, y_dev).wait_send()
        for p in range(2):
            move(2 * layer(j) + (1 - x), p, y_sem, y_dev).wait_send()


def fused(hidden, weight, momentum, gradient, indices, counts):
    tiles, side, cols = weight.shape
    kept_count = indices.shape[2]
    half = tiles * side
    own_tokens = hidden.shape[0]
    live = jnp.arange(kept_count, dtype=jnp.int32)[None, :] < counts[0][:, None]
    index = jnp.where(live, indices[0], -1).reshape(tiles, 2 * kept_count)
    index = jnp.concatenate([index, index], axis=1)
    table = np.kron(np.eye(4), cosine_table(side))
    basis = np.stack([table, table.T]).astype(np.float32)
    basis_high = basis.astype(jnp.bfloat16)
    basis_low = (basis - basis_high.astype(np.float32)).astype(jnp.bfloat16)
    vmem = pl.BlockSpec(memory_space=pltpu.VMEM)
    number = 8 * CHUNKS
    dma = pltpu.SemaphoreType.DMA
    keys, update, new_momentum = pl.pallas_call(
        fused_kernel,
        out_shape=(
            jax.ShapeDtypeStruct((own_tokens, 8 * cols), jnp.bfloat16),
            jax.ShapeDtypeStruct((tiles, side // 2, cols), jnp.bfloat16),
            jax.ShapeDtypeStruct(momentum.shape, jnp.float32),
        ),
        in_specs=[pl.BlockSpec(memory_space=pl.ANY)] + [vmem] * 7,
        out_specs=(vmem, vmem, vmem),
        scratch_shapes=[
            pltpu.VMEM((8, half, cols), jnp.bfloat16),
            pltpu.VMEM((2 * own_tokens, half), jnp.bfloat16),
            pltpu.VMEM((4, 2 * own_tokens, 2 * cols), jnp.float32),
            pltpu.VMEM((4, own_tokens, 2 * cols), jnp.float32),
            pltpu.VMEM((half, cols), jnp.float32),
            pltpu.VMEM((tiles, cols), jnp.float32),
            pltpu.VMEM((tiles, cols), jnp.float32),
            pltpu.VMEM((tiles, cols), jnp.int32),
            dma((number,)),
            dma((2, number)),
            dma((number,)),
            dma((number,)),
            dma((4,)),
            dma((3,)),
            dma((4,)),
            dma((4,)),
        ],
        compiler_params=pltpu.CompilerParams(
            collective_id=0, has_side_effects=True, vmem_limit_bytes=48 * 1024 * 1024
        ),
    )(
        hidden,
        weight,
        momentum,
        gradient,
        index,
        jnp.asarray(basis),
        jnp.asarray(basis_high),
        jnp.asarray(basis_low),
    )
    return keys, update, new_momentum


finest_numeric_accuracy = lax.Precision.HIGHEST


def dct_table(length):
    wave_number = jnp.arange(length, dtype=jnp.float32)[:, None]
    position = jnp.arange(length, dtype=jnp.float32)[None, :]
    dct_rows = jnp.cos(jnp.pi * (2.0 * position + 1.0) * wave_number / (2.0 * length)) * jnp.sqrt(
        2.0 / length
    )
    return jnp.where(wave_number == 0.0, dct_rows * jnp.sqrt(0.5), dct_rows)


def make_pair(dct_rows):
    empty_square_tile = jnp.zeros_like(dct_rows)
    upper_half = jnp.concatenate([dct_rows, empty_square_tile], axis=1)
    lower_half = jnp.concatenate([empty_square_tile, dct_rows], axis=1)
    return jnp.concatenate([upper_half, lower_half], axis=0)


def to_spectrum(tile_data, row_basis_operator, paired_cosine_matrix):
    partial_transform = jnp.einsum(
        "ka,tab->tkb", row_basis_operator, tile_data, precision=finest_numeric_accuracy
    )
    return jnp.einsum(
        "tkb,cb->tkc", partial_transform, paired_cosine_matrix, precision=finest_numeric_accuracy
    )


def from_spectrum(tile_frequency_coefficients, row_basis_operator, paired_cosine_matrix):
    partial_transform = jnp.einsum(
        "yh,kyi->khi",
        row_basis_operator,
        tile_frequency_coefficients,
        precision=finest_numeric_accuracy,
    )
    return jnp.einsum(
        "pln,ns->pls", partial_transform, paired_cosine_matrix, precision=finest_numeric_accuracy
    )


def plain(hidden, weight, momentum, gradient, indices, counts):
    tiles_dev, block_side, tile_cols = weight.shape
    kept_count = indices.shape[2]
    replicas = lax.axis_size("rep")
    group_size = lax.axis_size("fsdp")
    all_tiles = tiles_dev * group_size
    width = hidden.shape[1]
    dct_rows = dct_table(block_side)
    paired_cosine_matrix = make_pair(dct_rows)
    moment = decay_rate * momentum[0] + gradient[0].astype(jnp.float32)
    tile_frequency_coefficients = to_spectrum(moment, dct_rows, paired_cosine_matrix)
    span_ids = jnp.arange(2 * tiles_dev, dtype=jnp.int32)[:, None]
    places = (
        span_ids // 2 * (block_side * tile_cols)
        + indices[0] // block_side * tile_cols
        + span_ids % 2 * block_side
        + indices[0] % block_side
    )
    picked = tile_frequency_coefficients.reshape(-1)[places]
    is_live = jnp.arange(kept_count, dtype=jnp.int32)[None, :] < counts[0][:, None]
    kept_values = jnp.where(is_live, picked, jnp.zeros_like(picked))
    flat_size = tiles_dev * block_side * tile_cols
    own_spectra = (
        jnp.zeros((flat_size,), jnp.float32).at[places.reshape(-1)].add(kept_values.reshape(-1))
    )
    own_spectra = own_spectra.reshape(tiles_dev, block_side, tile_cols)
    new_momentum = (moment - from_spectrum(own_spectra, dct_rows, paired_cosine_matrix))[None]
    all_places, all_values = (
        lax.all_gather(places[None], "rep", axis=0, tiled=True),
        lax.all_gather(kept_values[None], "rep", axis=0, tiled=True),
    )
    shared = (
        jnp.zeros((flat_size,), jnp.float32).at[all_places.reshape(-1)].add(all_values.reshape(-1))
    )
    shared = shared.reshape(tiles_dev, block_side, tile_cols) / replicas
    energy = jnp.sum((shared * shared).reshape(tiles_dev, block_side, 2, block_side), axis=(1, 3))
    span_scale = jnp.sqrt(energy / (block_side * block_side) + tiny_eps)
    span_scale = jnp.repeat(span_scale, block_side, axis=1)[:, None, :]
    rows_rep = block_side // replicas
    row_first = lax.axis_index("rep") * rows_rep
    raw_descent_direction = from_spectrum(shared, dct_rows, paired_cosine_matrix)
    update = jnp.tanh(raw_descent_direction / span_scale).astype(jnp.bfloat16)
    revised_parameters = (
        weight.astype(jnp.float32) - step_size * update.astype(jnp.float32)
    ).astype(jnp.bfloat16)
    assembled = lax.all_gather(revised_parameters, "fsdp", axis=0, tiled=True)
    out_update = lax.dynamic_slice_in_dim(update, row_first, rows_rep, 1)
    out_blocks = all_tiles // (width // block_side)
    matrix = assembled.reshape(out_blocks, width // block_side, block_side, tile_cols).transpose(
        1, 2, 0, 3
    )
    matrix = matrix.reshape(width, out_blocks * tile_cols)
    key_states = jnp.dot(hidden, matrix, preferred_element_type=jnp.float32).astype(jnp.bfloat16)
    return (key_states, out_update, new_momentum)


def solution(mesh):
    in_specs = (
        P(("rep", "fsdp"), None),
        P("fsdp", None, None),
        P("rep", "fsdp", None, None),
        P("rep", "fsdp", None, None),
        P("rep", "fsdp", None),
        P("rep", "fsdp"),
    )
    out_specs = (P(("rep", "fsdp"), None), P("fsdp", "rep", None), P("rep", "fsdp", None, None))
    small = mesh.shape["rep"] == 2 and mesh.shape["fsdp"] == 16
    shards = fused if small else plain
    return jax.shard_map(shards, mesh=mesh, in_specs=in_specs, out_specs=out_specs, check_vma=False)
```

profile of v0, /device:TPU:7, one launch (start us, length us, event | category | flops | bytes accessed | tf_op | source)
XLA Modules:
  0.0 79.2 jit_solution(13881903747988128979)
XLA Ops:
  0.6 0.5 broadcast.7
  1.1 1.3 %reduce.3 = s32[80]{0:T(128)S(1)} reduce(s32[1,80]{1,0:T(1,128)} %param.14, s32[]{:T(128)} %broadcast.7), dimensions={0}, to_apply=%param.14.reduce_sub_computation.3 | reduce | bytes 644 | tf_op args[5]
  2.5 0.1 lt.23
  2.5 0.1 lt.25
  2.7 0.1 copy.13
  2.7 0.1 copy.14
  2.8 0.8 %copy.15 = s32[1,80,32]{2,1,0:T(8,128)S(1)} copy(s32[1,80,32]{1,2,0:T(8,128)} %param.13) | data formatting | bytes 20480 | tf_op args[4]
  3.6 0.1 squeeze.3
  3.7 0.1 pad_add_fusion.index
  3.8 0.0 copy-start
  3.8 1.3 %copy-done = f32[1,40,64,128]{3,2,1,0:T(8,128)S(1)} copy-done((f32[1,40,64,128]{3,2,1,0:T(8,128)S(1)}, f32[1,40,64,128]{3,2,1,0:T(8,128)}, u32[]{:S(2)}) %copy-start) | copy-done | bytes 1310744
  5.1 0.0 copy-start.1
  5.1 1.1 %copy-done.1 = bf16[40,64,128]{2,1,0:T(8,128)(2,1)S(1)} copy-done((bf16[40,64,128]{2,1,0:T(8,128)(2,1)S(1)}, bf16[40,64,128]{2,1,0:T(8,128)(2,1)}, u32[]{:S(2)}) %copy-start.1) | copy-done | bytes 655384
  6.2 0.0 copy-start.2
  6.2 1.1 %copy-done.2 = bf16[1,40,64,128]{3,2,1,0:T(8,128)(2,1)S(1)} copy-done((bf16[1,40,64,128]{3,2,1,0:T(8,128)(2,1)S(1)}, bf16[1,40,64,128]{3,2,1,0:T(8,128)(2,1)}, u32[]{:S(2)}) %copy-start.2) | copy-done | bytes 655384
  7.3 0.0 copy-start.3
  7.3 1.0 %copy-done.3 = f32[2,256,256]{2,1,0:T(8,128)S(1)} copy-done((f32[2,256,256]{2,1,0:T(8,128)S(1)}, f32[2,256,256]{2,1,0:T(8,128)}, u32[]{:S(2)}) %copy-start.3) | copy-done | bytes 524312
  8.3 0.0 copy-start.4
  8.3 0.9 %copy-done.4 = bf16[2,256,256]{2,1,0:T(8,128)(2,1)S(1)} copy-done((bf16[2,256,256]{2,1,0:T(8,128)(2,1)S(1)}, bf16[2,256,256]{2,1,0:T(8,128)(2,1)}, u32[]{:S(2)}) %copy-start.4) | copy-done | bytes 262168
  9.3 0.0 copy-start.5
  9.3 0.9 %copy-done.5 = bf16[2,256,256]{2,1,0:T(8,128)(2,1)S(1)} copy-done((bf16[2,256,256]{2,1,0:T(8,128)(2,1)S(1)}, bf16[2,256,256]{2,1,0:T(8,128)(2,1)}, u32[]{:S(2)}) %copy-start.5) | copy-done | bytes 262168
  10.2 66.4 %shard_map.112 = (bf16[256,1024]{1,0:T(8,128)(2,1)S(1)}, bf16[40,32,128]{2,1,0:T(8,128)(2,1)S(1)}, f32[1,40,64,128]{3,2,1,0:T(8,128)S(1)}) custom-call(bf16[256,5120]{1,0:T(8,128)(2,1)} %hidden.1, bf16[40,64,128]{2,1,0:T(8,128)(2,1)S(1)} %copy-done.1, f32[1,40,64,128]{3,2,1,0:T(8,128)S(1)} %copy-done, bf16[1,40,64,128]{3,2,1,0:T(8,128)(2,1)S(1)} %copy-done.2, ...), custom_call_target="tpu_custom_call" | custom-call | tf_op jit(solution)/shard_map/pallas_call | solution.py:384
  76.6 0.8 %copy.19 = bf16[256,1024]{1,0:T(8,128)(2,1)} copy(bf16[256,1024]{1,0:T(8,128)(2,1)S(1)} %get-tuple-element.6) | data formatting | bytes 1048576
  77.4 0.7 copy.20
  78.1 1.1 %copy.21 = f32[1,40,64,128]{3,2,1,0:T(8,128)} copy(f32[1,40,64,128]{3,2,1,0:T(8,128)S(1)} %get-tuple-element.8) | data formatting | bytes 2621440
  (3 shorter events, 0.0 us)
Async XLA Ops:
  3.8 1.3 %copy-start = (f32[1,40,64,128]{3,2,1,0:T(8,128)S(1)}, f32[1,40,64,128]{3,2,1,0:T(8,128)}, u32[]{:S(2)}) copy-start(f32[1,40,64,128]{3,2,1,0:T(8,128)} %momentum.1) | copy-start | bytes 3932164
  5.1 1.1 %copy-start.1 = (bf16[40,64,128]{2,1,0:T(8,128)(2,1)S(1)}, bf16[40,64,128]{2,1,0:T(8,128)(2,1)}, u32[]{:S(2)}) copy-start(bf16[40,64,128]{2,1,0:T(8,128)(2,1)} %weight.1) | copy-start | bytes 1966084
  6.2 1.1 %copy-start.2 = (bf16[1,40,64,128]{3,2,1,0:T(8,128)(2,1)S(1)}, bf16[1,40,64,128]{3,2,1,0:T(8,128)(2,1)}, u32[]{:S(2)}) copy-start(bf16[1,40,64,128]{3,2,1,0:T(8,128)(2,1)} %gradient.1) | copy-start | bytes 1966084
  7.3 1.0 %copy-start.3 = (f32[2,256,256]{2,1,0:T(8,128)S(1)}, f32[2,256,256]{2,1,0:T(8,128)}, u32[]{:S(2)}) copy-start(f32[2,256,256]{2,1,0:T(8,128)} %constant.8.clone.basis) | copy-start | bytes 1572868
  8.3 0.9 %copy-start.4 = (bf16[2,256,256]{2,1,0:T(8,128)(2,1)S(1)}, bf16[2,256,256]{2,1,0:T(8,128)(2,1)}, u32[]{:S(2)}) copy-start(bf16[2,256,256]{2,1,0:T(8,128)(2,1)} %constant.10.clone.basis_low) | copy-start | bytes 786436
  9.3 0.9 %copy-start.5 = (bf16[2,256,256]{2,1,0:T(8,128)(2,1)S(1)}, bf16[2,256,256]{2,1,0:T(8,128)(2,1)}, u32[]{:S(2)}) copy-start(bf16[2,256,256]{2,1,0:T(8,128)(2,1)} %constant.9.clone.basis_high) | copy-start | bytes 786436
where the time goes:
time: 80.2 us; the launch traced here: 79.2 us
  Pallas kernels  66.4 us (83%)
  local copies, waits for them, and re-layouts  10.8 us (13%)
  other arithmetic  1.4 us (2%)
    pallas_call x1, Pallas kernels, fused(): pl.pallas_call(fused_kernel, out_shape=(jax.ShapeDtypeStruct((own_tokens,...  66.4 us
    unnamed x17, local copies, waits for them, and re-layouts  10.3 us

commit v1 on v0

--- a/solution.py
+++ b/solution.py
@@ -36,25 +36,21 @@
     return lax.dot_general(a, b, (((1,), (1,)), ((), ())), preferred_element_type=jnp.float32)
 
 
-def right3(a, b_high, b_low):
-    high, low = split(a)
-    return dot(high, b_high) + (dot(high, b_low) + dot(low, b_high))
-
-
-def left3(a_high, a_low, b):
-    high, low = split(b)
-    return dot(a_high, high) + (dot(a_high, low) + dot(a_low, high))
+def split3(value):
+    high = value.astype(jnp.bfloat16)
+    rest = value - high.astype(jnp.float32)
+    middle = rest.astype(jnp.bfloat16)
+    return high, middle, (rest - middle.astype(jnp.float32)).astype(jnp.bfloat16)
 
 
 def fused_kernel(
     hidden,
-    weight,
-    momentum,
-    gradient,
-    index,
-    basis,
-    basis_high,
-    basis_low,
+    weight_hbm,
+    momentum_hbm,
+    gradient_hbm,
+    indices,
+    counts,
+    basis_hbm,
     keys,
     update,
     new_momentum,
@@ -66,15 +62,41 @@
     kept,
     kept_other,
     index_other,
+    index,
+    weight,
+    momentum,
+    gradient,
+    basis,
+    raw_index,
+    raw_count,
+    spread,
+    load_sem,
     recv_sem,
     z_sem,
     x_sem,
     y_sem,
     small_send,
     small_recv,
+    kept_send,
+    kept_recv,
     part_send,
     part_recv,
 ):
+    loads = [
+        pltpu.make_async_copy(src, dst, load_sem.at[n])
+        for n, (src, dst) in enumerate(
+            (
+                (indices.at[0], raw_index),
+                (counts, raw_count),
+                (basis_hbm, basis),
+                (momentum_hbm.at[0], momentum),
+                (gradient_hbm.at[0], gradient),
+                (weight_hbm, weight),
+            )
+        )
+    ]
+    for load in loads:
+        load.start()
     tiles, side, cols = weight.shape
     per = tiles // CHUNKS
     rows = per * side
@@ -113,8 +135,6 @@
             src_ref=src, dst_ref=dst, send_sem=send, recv_sem=recv, device_id=device, device_id_type=MESH
         )
 
-    index_copy = remote(index, index_other, small_send.at[0], small_recv.at[0], y_dev)
-    index_copy.start()
     token_copy = remote(
         hidden.at[:, pl.ds(pl.multiple_of((1 - c) * half, 128), half)],
         tokens.at[pl.ds(own_tokens, own_tokens)],
@@ -173,26 +193,42 @@
         return jnp.concatenate([value[:, :cols], value[:, cols:]], axis=0)
 
     def inverse(coefficients):
-        part = right3(coefficients, basis_high[0, :pair, :pair], basis_low[0, :pair, :pair])
-        return stacked(left3(basis_high[1], basis_low[1], both_halves(part)))
+        one, two = split(both_halves(coefficients))
+        part = dot(one, basis[0]) + (dot(one, basis[1]) + dot(two, basis[0]))
+        one, two = split(part)
+        return stacked(dot(basis[3], one) + (dot(basis[3], two) + dot(basis[4], one)))
+
+    def transform(value):
+        one, two, three = split3(both_halves(value))
+        part = dot(one, basis[3]) + (
+            (dot(one, basis[4]) + dot(two, basis[3]))
+            + (dot(one, basis[5]) + dot(two, basis[4]) + dot(three, basis[3]))
+        )
+        one, two, three = split3(part)
+        return stacked(
+            dot(basis[0], one)
+            + (
+                (dot(basis[0], two) + dot(basis[1], one))
+                + (dot(basis[0], three) + dot(basis[1], two) + dot(basis[2], one))
+            )
+        )
 
     def tile_slice(q):
-        return pl.ds(pl.multiple_of(q * per, per), per)
-
-    def forward(q, carry):
+        return pl.ds(q * per if isinstance(q, int) else pl.multiple_of(q * per, per), per)
+
+    def row_slice(q):
+        return pl.ds(q * rows if isinstance(q, int) else pl.multiple_of(q * rows, rows), rows)
+
+    def kept_copy(q):
         here = tile_slice(q)
-        moment = decay_rate * momentum[0, here] + gradient[0, here].astype(jnp.float32)
+        return remote(kept.at[here], kept_other.at[here], kept_send.at[q], kept_recv.at[q], y_dev)
+
+    def forward(q):
+        here = tile_slice(q)
+        moment = decay_rate * momentum[here] + gradient[here].astype(jnp.float32)
         new_momentum[0, here] = moment
-        part = jnp.dot(
-            moment.reshape(rows, cols),
-            basis[1, :pair, :pair],
-            precision=exact,
-            preferred_element_type=jnp.float32,
-        )
-        spectrum = stacked(
-            jnp.dot(basis[0], both_halves(part), precision=exact, preferred_element_type=jnp.float32)
-        )
-        spectra[pl.ds(pl.multiple_of(q * rows, rows), rows)] = spectrum
+        spectrum = transform(moment.reshape(rows, cols))
+        spectra[row_slice(q)] = spectrum
         idx = index[here]
         found = []
         for t in range(per):
@@ -202,19 +238,14 @@
             taken = taken[:side] + taken[side:]
             found.append(jnp.sum(jnp.where(hot_rows(one), taken, 0.0), axis=0, keepdims=True))
         kept[here] = jnp.concatenate(found, axis=0)
-        return carry
-
-    lax.fori_loop(0, CHUNKS, forward, 0)
-    kept_copy = remote(kept, kept_other, small_send.at[2], small_recv.at[2], y_dev)
-    kept_copy.start()
-    index_copy.wait_recv()
-    kept_copy.wait_recv()
+        kept_copy(q).start()
 
     own_block = 2 * z + x
 
-    def step(p, carry):
+    def step(p):
         q = place(p)
         here = tile_slice(q)
+        kept_copy(q).wait_recv()
         idx = jnp.where(left_lanes, index[here], index_other[here])
         values = jnp.where(left_lanes, kept[here], kept_other[here]) * 0.5
         dense = []
@@ -234,30 +265,56 @@
         shown = jnp.where(r == 0, tiled[:, : side // 2], tiled[:, side // 2 :])
         update[here] = shown.astype(jnp.bfloat16)
         old = weight[here].astype(jnp.float32).reshape(rows, cols)
-        blocks[own_block, pl.ds(pl.multiple_of(q * rows, rows), rows)] = (
-            old - step_size * direction
-        ).astype(jnp.bfloat16)
-
-        @pl.when(jnp.logical_and(up_ok, p < 4))
-        def _():
-            z_move(own_block, p, 0).start()
-
-        @pl.when(jnp.logical_and(down_ok, p < 4))
-        def _():
-            z_move(own_block, p, 1).start()
-
-        @pl.when(p < 3)
-        def _():
+        blocks[own_block, row_slice(q)] = (old - step_size * direction).astype(jnp.bfloat16)
+
+        if p < 4:
+
+            @pl.when(up_ok)
+            def _():
+                z_move(own_block, p, 0).start()
+
+            @pl.when(down_ok)
+            def _():
+                z_move(own_block, p, 1).start()
+
+        if p < 3:
             move(own_block, p, x_sem, x_dev).start()
 
-        return carry
-
-    lax.fori_loop(0, CHUNKS, step, 0)
+    loads[0].wait()
+    loads[1].wait()
+    spans = 2 * tiles
+    diagonal = lax.broadcasted_iota(jnp.int32, (spans, spans), 0) == lax.broadcasted_iota(
+        jnp.int32, (spans, spans), 1
+    )
+    limit = jnp.sum(jnp.where(diagonal, raw_count[...].astype(jnp.float32), 0.0), axis=1, keepdims=True)
+    listed = raw_index[...]
+    position = lax.broadcasted_iota(jnp.int32, listed.shape, 1).astype(jnp.float32)
+    listed = jnp.where(position < limit, listed, -1)
+    spread[...] = jnp.concatenate([listed] * 4, axis=1)
+    index[...] = jnp.where(
+        second > 0, spread[pl.ds(1, tiles, stride=2)], spread[pl.ds(0, tiles, stride=2)]
+    )
+    index_copy = remote(index, index_other, small_send.at[0], small_recv.at[0], y_dev)
+    index_copy.start()
+    for load in loads[2:5]:
+        load.wait()
+    forward(0)
+    forward(CHUNKS - 1)
+    forward(1)
+    loads[5].wait()
+    index_copy.wait_recv()
+    step(0)
+    forward(3)
+    step(1)
+    forward(2)
+    step(2)
+    step(3)
+    step(4)
 
     def settle(q, carry):
         here = tile_slice(q)
         idx = index[here]
-        spectrum = spectra[pl.ds(pl.multiple_of(q * rows, rows), rows)]
+        spectrum = spectra[row_slice(q)]
         masks = []
         for t in range(per):
             one = idx[t : t + 1]
@@ -340,7 +397,8 @@
 
     index_copy.wait_send()
     token_copy.wait_send()
-    kept_copy.wait_send()
+    for q in range(CHUNKS):
+        kept_copy(q).wait_send()
     for j in range(4):
         part_copy(j).wait_send()
         o = 2 * layer(j) + x
@@ -368,16 +426,15 @@
 
 def fused(hidden, weight, momentum, gradient, indices, counts):
     tiles, side, cols = weight.shape
-    kept_count = indices.shape[2]
     half = tiles * side
     own_tokens = hidden.shape[0]
-    live = jnp.arange(kept_count, dtype=jnp.int32)[None, :] < counts[0][:, None]
-    index = jnp.where(live, indices[0], -1).reshape(tiles, 2 * kept_count)
-    index = jnp.concatenate([index, index], axis=1)
     table = np.kron(np.eye(4), cosine_table(side))
-    basis = np.stack([table, table.T]).astype(np.float32)
-    basis_high = basis.astype(jnp.bfloat16)
-    basis_low = (basis - basis_high.astype(np.float32)).astype(jnp.bfloat16)
+    parts = []
+    for rest in (table, table.T):
+        for _ in range(3):
+            parts.append(rest.astype(jnp.bfloat16))
+            rest = rest - parts[-1].astype(np.float64)
+    basis = jnp.asarray(np.stack(parts))
     vmem = pl.BlockSpec(memory_space=pltpu.VMEM)
     number = 8 * CHUNKS
     dma = pltpu.SemaphoreType.DMA
@@ -388,7 +445,7 @@
             jax.ShapeDtypeStruct((tiles, side // 2, cols), jnp.bfloat16),
             jax.ShapeDtypeStruct(momentum.shape, jnp.float32),
         ),
-        in_specs=[pl.BlockSpec(memory_space=pl.ANY)] + [vmem] * 7,
+        in_specs=[pl.BlockSpec(memory_space=pl.ANY)] * 7,
         out_specs=(vmem, vmem, vmem),
         scratch_shapes=[
             pltpu.VMEM((8, half, cols), jnp.bfloat16),
@@ -399,27 +456,37 @@
             pltpu.VMEM((tiles, cols), jnp.float32),
             pltpu.VMEM((tiles, cols), jnp.float32),
             pltpu.VMEM((tiles, cols), jnp.int32),
+            pltpu.VMEM((tiles, cols), jnp.int32),
+            pltpu.VMEM(weight.shape, weight.dtype),
+            pltpu.VMEM(momentum.shape[1:], momentum.dtype),
+            pltpu.VMEM(gradient.shape[1:], gradient.dtype),
+            pltpu.VMEM(basis.shape, basis.dtype),
+            pltpu.VMEM(indices.shape[1:], indices.dtype),
+            pltpu.VMEM(counts.shape, counts.dtype),
+            pltpu.VMEM((2 * tiles, cols), jnp.int32),
+            dma((6,)),
             dma((number,)),
             dma((2, number)),
             dma((number,)),
             dma((number,)),
             dma((4,)),
             dma((3,)),
+            dma((CHUNKS,)),
+            dma((CHUNKS,)),
             dma((4,)),
             dma((4,)),
         ],
         compiler_params=pltpu.CompilerParams(
-            collective_id=0, has_side_effects=True, vmem_limit_bytes=48 * 1024 * 1024
+            collective_id=0, has_side_effects=True, vmem_limit_bytes=60 * 1024 * 1024
         ),
     )(
         hidden,
         weight,
         momentum,
         gradient,
-        index,
-        jnp.asarray(basis),
-        jnp.asarray(basis_high),
-        jnp.asarray(basis_low),
+        indices,
+        counts,
+        basis,
     )
     return keys, update, new_momentum
 

time: 80.2 us -> 76.6 us (0.955)
  local copies, waits for them, and re-layouts: 10.8 us -> 6.17 us
  Pallas kernels: 66.4 us -> 68.7 us
  other arithmetic: 1.4 us -> 0 us
    unnamed x17 -> x6, local copies, waits for them, and re-layouts: 10.3 us -> 6.17 us
    pallas_call x1, Pallas kernels: 66.4 us -> 68.7 us  [fused(): pl.pallas_call(fused_kernel, out_shape=(jax.ShapeDtypeStruct((own_tokens,...]
    unnamed x1 -> x0, other arithmetic: 1.32 us -> none
where the time goes in v1:
time: 76.6 us; the launch traced here: 75.5 us
  Pallas kernels  68.7 us (90%)
  local copies, waits for them, and re-layouts  6.17 us (8%)
    pallas_call x1, Pallas kernels, fused(): pl.pallas_call(fused_kernel, out_shape=(jax.ShapeDtypeStruct((own_tokens,...  68.7 us
    unnamed x6, local copies, waits for them, and re-layouts  6.17 us

profile of v1, /device:TPU:7, one launch (start us, length us, event | category | flops | bytes accessed | tf_op | source)
XLA Modules:
  0.0 75.5 jit_solution(14550239092477409291)
XLA Ops:
  0.6 1.4 %copy.10.indices = s32[1,80,32]{2,1,0:T(8,128)} copy(s32[1,80,32]{1,2,0:T(8,128)} %param.11) | data formatting | bytes 20480 | tf_op args[4]
  2.1 68.7 %shard_map.94 = (bf16[256,1024]{1,0:T(8,128)(2,1)}, bf16[40,32,128]{2,1,0:T(8,128)(2,1)}, f32[1,40,64,128]{3,2,1,0:T(8,128)}) custom-call(bf16[256,5120]{1,0:T(8,128)(2,1)} %hidden.1, bf16[40,64,128]{2,1,0:T(8,128)(2,1)} %weight_hbm.1, f32[1,40,64,128]{3,2,1,0:T(8,128)} %momentum_hbm.1, bf16[1,40,64,128]{3,2,1,0:T(8,128)(2,1)} %gradient_hbm.1, ...), custom_call_target="tpu_custom_call" | custom-call | tf_op jit(solution)/shard_map/pallas_call | solution.py:441
  70.7 0.0 copy-start
  70.7 2.0 %copy.14 = bf16[256,1024]{1,0:T(8,128)(2,1)} copy(bf16[256,1024]{1,0:T(8,128)(2,1)} %get-tuple-element.6) | data formatting | bytes 1048576
  72.7 1.7 %copy.15 = bf16[40,32,128]{2,1,0:T(8,128)(2,1)} copy(bf16[40,32,128]{2,1,0:T(8,128)(2,1)} %get-tuple-element.7) | data formatting | bytes 655360
  74.4 0.0 copy-done
  74.4 1.1 %copy.16 = f32[1,40,64,128]{3,2,1,0:T(8,128)} copy(f32[1,40,64,128]{3,2,1,0:T(8,128)S(1)} %copy-done) | data formatting | bytes 2621440
Async XLA Ops:
  70.7 3.7 %copy-start = (f32[1,40,64,128]{3,2,1,0:T(8,128)S(1)}, f32[1,40,64,128]{3,2,1,0:T(8,128)}, u32[]{:S(2)}) copy-start(f32[1,40,64,128]{3,2,1,0:T(8,128)} %get-tuple-element.8) | copy-start | bytes 3932164

commit v2 on v1

--- a/solution.py
+++ b/solution.py
@@ -280,17 +280,52 @@
         if p < 3:
             move(own_block, p, x_sem, x_dev).start()
 
+    def arrived(o, p):
+        move(o, p, x_sem, x_dev).wait_recv()
+
+    def from_z(j, p):
+        o = 2 * layer(j) + x
+        arrived(o, p)
+        below = layer(j) < z
+
+        @pl.when(jnp.logical_and(below, up_ok))
+        def _():
+            z_move(o, p, 0).start()
+
+        @pl.when(jnp.logical_and(jnp.logical_not(below), down_ok))
+        def _():
+            z_move(o, p, 1).start()
+
+        if p < 3:
+            move(o, p, x_sem, x_dev).start()
+        if p == 0:
+            move(o, p, y_sem, y_dev).start()
+
+    def from_x(j, p):
+        o = 2 * layer(j) + (1 - x)
+        arrived(o, p)
+        if p < 2:
+            move(o, p, y_sem, y_dev).start()
+
+    def settle(q):
+        here = tile_slice(q)
+        idx = index[here]
+        spectrum = spectra[row_slice(q)]
+        masks = []
+        for t in range(per):
+            one = idx[t : t + 1]
+            hot = jnp.where(jnp.logical_and(hot_rows(one), left_lanes), 1.0, 0.0).astype(jnp.bfloat16)
+            masks.append(dot_nt(hot, hot_cols(one)))
+        own = jnp.where(jnp.concatenate(masks, axis=0) > 0.5, spectrum, 0.0)
+        new_momentum[0, here] = new_momentum[0, here] - inverse(own).reshape(per, side, cols)
+
     loads[0].wait()
     loads[1].wait()
-    spans = 2 * tiles
-    diagonal = lax.broadcasted_iota(jnp.int32, (spans, spans), 0) == lax.broadcasted_iota(
-        jnp.int32, (spans, spans), 1
-    )
-    limit = jnp.sum(jnp.where(diagonal, raw_count[...].astype(jnp.float32), 0.0), axis=1, keepdims=True)
     listed = raw_index[...]
-    position = lax.broadcasted_iota(jnp.int32, listed.shape, 1).astype(jnp.float32)
-    listed = jnp.where(position < limit, listed, -1)
-    spread[...] = jnp.concatenate([listed] * 4, axis=1)
+    position = lax.broadcasted_iota(jnp.int32, listed.shape, 0)
+    spread[...] = jnp.full(spread.shape, -1, jnp.int32)
+    spread[: listed.shape[0], : listed.shape[1]] = jnp.where(position < raw_count[...], listed, -1)
+    spread[...] = jnp.transpose(jnp.concatenate([spread[: listed.shape[0]]] * 4, axis=0))
     index[...] = jnp.where(
         second > 0, spread[pl.ds(1, tiles, stride=2)], spread[pl.ds(0, tiles, stride=2)]
     )
@@ -306,54 +341,20 @@
     step(0)
     forward(3)
     step(1)
+    from_z(1, 0)
+    from_x(0, 0)
     forward(2)
     step(2)
+    from_z(1, 1)
+    from_x(0, 1)
     step(3)
+    from_z(1, 2)
+    from_x(0, 2)
     step(4)
-
-    def settle(q, carry):
-        here = tile_slice(q)
-        idx = index[here]
-        spectrum = spectra[row_slice(q)]
-        masks = []
-        for t in range(per):
-            one = idx[t : t + 1]
-            hot = jnp.where(jnp.logical_and(hot_rows(one), left_lanes), 1.0, 0.0).astype(jnp.bfloat16)
-            masks.append(dot_nt(hot, hot_cols(one)))
-        own = jnp.where(jnp.concatenate(masks, axis=0) > 0.5, spectrum, 0.0)
-        new_momentum[0, here] = new_momentum[0, here] - inverse(own).reshape(per, side, cols)
-        return carry
-
-    lax.fori_loop(0, CHUNKS, settle, 0)
+    from_z(1, 3)
+
     token_local.wait()
     token_copy.wait_recv()
-
-    def arrived(o, p):
-        move(o, p, x_sem, x_dev).wait_recv()
-
-    def from_z(j, p):
-        o = 2 * layer(j) + x
-        arrived(o, p)
-        below = layer(j) < z
-
-        @pl.when(jnp.logical_and(below, up_ok))
-        def _():
-            z_move(o, p, 0).start()
-
-        @pl.when(jnp.logical_and(jnp.logical_not(below), down_ok))
-        def _():
-            z_move(o, p, 1).start()
-
-        if p < 3:
-            move(o, p, x_sem, x_dev).start()
-        if p == 0:
-            move(o, p, y_sem, y_dev).start()
-
-    def from_x(j, p):
-        o = 2 * layer(j) + (1 - x)
-        arrived(o, p)
-        if p < 2:
-            move(o, p, y_sem, y_dev).start()
 
     def part_copy(j):
         return remote(
@@ -377,18 +378,19 @@
         lax.fori_loop(1, CHUNKS, add, 0)
         part_copy(j).start()
 
-    for j in range(5):
-        for p in range(4):
-            if 1 <= j + 1 <= 3:
-                from_z(j + 1, p)
-            if j < 4 and p < 3:
-                from_x(j, p)
-        if j < 4:
-            if j > 0:
-                arrived(2 * layer(j) + x, 4)
-            arrived(2 * layer(j) + (1 - x), 4)
-            arrived(2 * layer(j) + (1 - x), 3)
-            multiply(j)
+    for j in range(4):
+        if j > 0:
+            for p in range(4):
+                if j < 3:
+                    from_z(j + 1, p)
+                if p < 3:
+                    from_x(j, p)
+                if j < 3 and 4 * (j - 1) + p < CHUNKS:
+                    settle(4 * (j - 1) + p)
+            arrived(2 * layer(j) + x, 4)
+        arrived(2 * layer(j) + (1 - x), 4)
+        arrived(2 * layer(j) + (1 - x), 3)
+        multiply(j)
 
     for j in range(4):
         part_copy(j).wait_recv()
@@ -426,6 +428,7 @@
 
 def fused(hidden, weight, momentum, gradient, indices, counts):
     tiles, side, cols = weight.shape
+    kept_count = indices.shape[2]
     half = tiles * side
     own_tokens = hidden.shape[0]
     table = np.kron(np.eye(4), cosine_table(side))
@@ -445,7 +448,7 @@
             jax.ShapeDtypeStruct((tiles, side // 2, cols), jnp.bfloat16),
             jax.ShapeDtypeStruct(momentum.shape, jnp.float32),
         ),
-        in_specs=[pl.BlockSpec(memory_space=pl.ANY)] * 7,
+        in_specs=[pl.BlockSpec(memory_space=pltpu.HBM)] * 7,
         out_specs=(vmem, vmem, vmem),
         scratch_shapes=[
             pltpu.VMEM((8, half, cols), jnp.bfloat16),
@@ -461,9 +464,9 @@
             pltpu.VMEM(momentum.shape[1:], momentum.dtype),
             pltpu.VMEM(gradient.shape[1:], gradient.dtype),
             pltpu.VMEM(basis.shape, basis.dtype),
-            pltpu.VMEM(indices.shape[1:], indices.dtype),
+            pltpu.VMEM((kept_count, 2 * tiles), indices.dtype),
             pltpu.VMEM(counts.shape, counts.dtype),
-            pltpu.VMEM((2 * tiles, cols), jnp.int32),
+            pltpu.VMEM((cols, cols), jnp.int32),
             dma((6,)),
             dma((number,)),
             dma((2, number)),
@@ -477,14 +480,14 @@
             dma((4,)),
         ],
         compiler_params=pltpu.CompilerParams(
-            collective_id=0, has_side_effects=True, vmem_limit_bytes=60 * 1024 * 1024
+            collective_id=0, has_side_effects=True, vmem_limit_bytes=53 * 1024 * 1024
         ),
     )(
         hidden,
         weight,
         momentum,
         gradient,
-        indices,
+        jnp.swapaxes(indices, 1, 2),
         counts,
         basis,
     )

time: 76.6 us -> 73.1 us (0.954)
  the two profiles are of different devices: /device:TPU:7 before, /device:TPU:1 now
where the time goes in v2:
time: 73.1 us; the launch traced here: 72.8 us
  Pallas kernels  68.2 us (93%)
  local copies, waits for them, and re-layouts  3.95 us (5%)
    pallas_call x1, Pallas kernels, fused(): pl.pallas_call(fused_kernel, out_shape=(jax.ShapeDtypeStruct((own_tokens,...  68.2 us
    unnamed x9, local copies, waits for them, and re-layouts  3.95 us

profile of v2, /device:TPU:1, one launch (start us, length us, event | category | flops | bytes accessed | tf_op | source)
XLA Modules:
  0.0 72.8 jit_solution(1838840258000863475)
XLA Ops:
  0.6 0.0 copy-start
  0.6 0.7 copy-done
  1.4 0.0 copy-start.1
  1.4 0.7 copy-done.1
  2.0 68.2 %shard_map.94 = (bf16[256,1024]{1,0:T(8,128)(2,1)S(1)}, bf16[40,32,128]{2,1,0:T(8,128)(2,1)S(1)}, f32[1,40,64,128]{3,2,1,0:T(8,128)}) custom-call(bf16[256,5120]{1,0:T(8,128)(2,1)} %hidden.1, bf16[40,64,128]{2,1,0:T(8,128)(2,1)} %weight_hbm.1, f32[1,40,64,128]{3,2,1,0:T(8,128)} %momentum_hbm.1, bf16[1,40,64,128]{3,2,1,0:T(8,128)(2,1)} %gradient_hbm.1, ...), custom_call_target="tpu_custom_call" | custom-call | tf_op jit(solution)/shard_map/pallas_call | solution.py:444
  70.2 0.0 copy-start.2
  70.2 0.8 %copy.13 = bf16[256,1024]{1,0:T(8,128)(2,1)} copy(bf16[256,1024]{1,0:T(8,128)(2,1)S(1)} %get-tuple-element.6) | data formatting | bytes 1048576
  71.0 0.7 copy.14
  71.7 0.0 copy-done.2
  71.8 1.1 %copy.15 = f32[1,40,64,128]{3,2,1,0:T(8,128)} copy(f32[1,40,64,128]{3,2,1,0:T(8,128)S(1)} %copy-done.2) | data formatting | bytes 2621440
Async XLA Ops:
  0.6 0.7 copy-start
  1.4 0.7 copy-start.1
  70.2 1.5 %copy-start.2 = (f32[1,40,64,128]{3,2,1,0:T(8,128)S(1)}, f32[1,40,64,128]{3,2,1,0:T(8,128)}, u32[]{:S(2)}) copy-start(f32[1,40,64,128]{3,2,1,0:T(8,128)} %get-tuple-element.8) | copy-start | bytes 3932164

commit v3 on v2

--- a/solution.py
+++ b/solution.py
@@ -283,10 +283,10 @@
     def arrived(o, p):
         move(o, p, x_sem, x_dev).wait_recv()
 
-    def from_z(j, p):
-        o = 2 * layer(j) + x
+    def from_z(level, p):
+        o = 2 * level + x
         arrived(o, p)
-        below = layer(j) < z
+        below = level < z
 
         @pl.when(jnp.logical_and(below, up_ok))
         def _():
@@ -318,6 +318,21 @@
             masks.append(dot_nt(hot, hot_cols(one)))
         own = jnp.where(jnp.concatenate(masks, axis=0) > 0.5, spectrum, 0.0)
         new_momentum[0, here] = new_momentum[0, here] - inverse(own).reshape(per, side, cols)
+
+    def near(p):
+        from_z(layer(1), p)
+
+        @pl.when(middle)
+        def _():
+            from_z(layer(2), p)
+
+    def far(p):
+        from_z(jnp.where(middle, layer(3), layer(2)), p)
+
+    def farthest(p):
+        @pl.when(jnp.logical_not(middle))
+        def _():
+            from_z(layer(3), p)
 
     loads[0].wait()
     loads[1].wait()
@@ -341,17 +356,17 @@
     step(0)
     forward(3)
     step(1)
-    from_z(1, 0)
+    near(0)
     from_x(0, 0)
     forward(2)
     step(2)
-    from_z(1, 1)
+    near(1)
     from_x(0, 1)
     step(3)
-    from_z(1, 2)
+    near(2)
     from_x(0, 2)
     step(4)
-    from_z(1, 3)
+    near(3)
 
     token_local.wait()
     token_copy.wait_recv()
@@ -382,7 +397,7 @@
         if j > 0:
             for p in range(4):
                 if j < 3:
-                    from_z(j + 1, p)
+                    (far, farthest)[j - 1](p)
                 if p < 3:
                     from_x(j, p)
                 if j < 3 and 4 * (j - 1) + p < CHUNKS:

time: 73.1 us -> 74.2 us (1.015)
  the two profiles are of different devices: /device:TPU:1 before, /device:TPU:7 now
where the time goes in v3:
time: 74.2 us; the launch traced here: 73.8 us
  Pallas kernels  69.2 us (93%)
  local copies, waits for them, and re-layouts  3.95 us (5%)
    pallas_call x1, Pallas kernels, fused(): pl.pallas_call(fused_kernel, out_shape=(jax.ShapeDtypeStruct((own_tokens,...  69.2 us
    unnamed x9, local copies, waits for them, and re-layouts  3.95 us

profile of v3, /device:TPU:7, one launch (start us, length us, event | category | flops | bytes accessed | tf_op | source)
XLA Modules:
  0.0 73.8 jit_solution(3294715456376627999)
XLA Ops:
  0.6 0.0 copy-start
  0.6 0.7 copy-done
  1.4 0.0 copy-start.1
  1.4 0.7 copy-done.1
  2.0 69.2 %shard_map.94 = (bf16[256,1024]{1,0:T(8,128)(2,1)S(1)}, bf16[40,32,128]{2,1,0:T(8,128)(2,1)S(1)}, f32[1,40,64,128]{3,2,1,0:T(8,128)}) custom-call(bf16[256,5120]{1,0:T(8,128)(2,1)} %hidden.1, bf16[40,64,128]{2,1,0:T(8,128)(2,1)} %weight_hbm.1, f32[1,40,64,128]{3,2,1,0:T(8,128)} %momentum_hbm.1, bf16[1,40,64,128]{3,2,1,0:T(8,128)(2,1)} %gradient_hbm.1, ...), custom_call_target="tpu_custom_call" | custom-call | tf_op jit(solution)/shard_map/pallas_call | solution.py:459
  71.3 0.0 copy-start.2
  71.3 0.8 %copy.13 = bf16[256,1024]{1,0:T(8,128)(2,1)} copy(bf16[256,1024]{1,0:T(8,128)(2,1)S(1)} %get-tuple-element.6) | data formatting | bytes 1048576
  72.1 0.7 copy.14
  72.8 0.0 copy-done.2
  72.8 1.1 %copy.15 = f32[1,40,64,128]{3,2,1,0:T(8,128)} copy(f32[1,40,64,128]{3,2,1,0:T(8,128)S(1)} %copy-done.2) | data formatting | bytes 2621440
Async XLA Ops:
  0.6 0.7 copy-start
  1.4 0.7 copy-start.1
  71.3 1.5 %copy-start.2 = (f32[1,40,64,128]{3,2,1,0:T(8,128)S(1)}, f32[1,40,64,128]{3,2,1,0:T(8,128)}, u32[]{:S(2)}) copy-start(f32[1,40,64,128]{3,2,1,0:T(8,128)} %get-tuple-element.8) | copy-start | bytes 3932164

commit v4 on v3

--- a/solution.py
+++ b/solution.py
@@ -13,7 +13,9 @@
 tiny_eps = 1e-06
 exact = lax.Precision.HIGHEST
 MESH = pl.DeviceIdType.MESH
-CHUNKS = 5
+CHUNKS = 10
+Z_CHUNKS = 8
+X_CHUNKS = 6
 
 
 def cosine_table(length):
@@ -104,6 +106,7 @@
     own_tokens = hidden.shape[0]
     pair = 2 * side
     four = 4 * side
+    wide = cols * rows // four
 
     r = lax.axis_index("rep")
     f = lax.axis_index("fsdp")
@@ -142,13 +145,11 @@
         small_recv.at[1],
         sib_dev,
     )
-    token_copy.start()
     token_local = pltpu.make_async_copy(
         hidden.at[:, pl.ds(pl.multiple_of(c * half, 128), half)],
         tokens.at[pl.ds(0, own_tokens)],
         small_send.at[3],
     )
-    token_local.start()
 
     def place(p):
         return jnp.where(r == 0, p, CHUNKS - 1 - p)
@@ -187,22 +188,24 @@
         return (col_iota == ((idx & (side - 1)) + second)).astype(jnp.bfloat16)
 
     def both_halves(value):
-        return jnp.concatenate([value[:four], value[four:]], axis=1)
+        return value if rows == four else jnp.concatenate([value[:four], value[four:]], axis=1)
 
     def stacked(value):
-        return jnp.concatenate([value[:, :cols], value[:, cols:]], axis=0)
+        return value if rows == four else jnp.concatenate([value[:, :cols], value[:, cols:]], axis=0)
 
     def inverse(coefficients):
         one, two = split(both_halves(coefficients))
-        part = dot(one, basis[0]) + (dot(one, basis[1]) + dot(two, basis[0]))
+        right = [basis[n, :wide, :wide] for n in (0, 1)]
+        part = dot(one, right[0]) + (dot(one, right[1]) + dot(two, right[0]))
         one, two = split(part)
         return stacked(dot(basis[3], one) + (dot(basis[3], two) + dot(basis[4], one)))
 
     def transform(value):
         one, two, three = split3(both_halves(value))
-        part = dot(one, basis[3]) + (
-            (dot(one, basis[4]) + dot(two, basis[3]))
-            + (dot(one, basis[5]) + dot(two, basis[4]) + dot(three, basis[3]))
+        right = [basis[n, :wide, :wide] for n in (3, 4, 5)]
+        part = dot(one, right[0]) + (
+            (dot(one, right[1]) + dot(two, right[0]))
+            + (dot(one, right[2]) + dot(two, right[1]) + dot(three, right[0]))
         )
         one, two, three = split3(part)
         return stacked(
@@ -220,8 +223,7 @@
         return pl.ds(q * rows if isinstance(q, int) else pl.multiple_of(q * rows, rows), rows)
 
     def kept_copy(q):
-        here = tile_slice(q)
-        return remote(kept.at[here], kept_other.at[here], kept_send.at[q], kept_recv.at[q], y_dev)
+        return remote(kept.at[q], kept_other.at[q], kept_send.at[q], kept_recv.at[q], y_dev)
 
     def forward(q):
         here = tile_slice(q)
@@ -229,7 +231,7 @@
         new_momentum[0, here] = moment
         spectrum = transform(moment.reshape(rows, cols))
         spectra[row_slice(q)] = spectrum
-        idx = index[here]
+        idx = index[q]
         found = []
         for t in range(per):
             one = idx[t : t + 1]
@@ -237,7 +239,7 @@
             taken = dot(jnp.concatenate([high, low], axis=0), hot_cols(one))
             taken = taken[:side] + taken[side:]
             found.append(jnp.sum(jnp.where(hot_rows(one), taken, 0.0), axis=0, keepdims=True))
-        kept[here] = jnp.concatenate(found, axis=0)
+        kept[q, :per] = jnp.concatenate(found, axis=0)
         kept_copy(q).start()
 
     own_block = 2 * z + x
@@ -246,8 +248,8 @@
         q = place(p)
         here = tile_slice(q)
         kept_copy(q).wait_recv()
-        idx = jnp.where(left_lanes, index[here], index_other[here])
-        values = jnp.where(left_lanes, kept[here], kept_other[here]) * 0.5
+        idx = jnp.where(left_lanes, index[q], index_other[q])
+        values = jnp.where(left_lanes, kept[q], kept_other[q]) * 0.5
         dense = []
         for t in range(per):
             one = idx[t : t + 1]
@@ -267,7 +269,7 @@
         old = weight[here].astype(jnp.float32).reshape(rows, cols)
         blocks[own_block, row_slice(q)] = (old - step_size * direction).astype(jnp.bfloat16)
 
-        if p < 4:
+        if p < Z_CHUNKS:
 
             @pl.when(up_ok)
             def _():
@@ -277,7 +279,7 @@
             def _():
                 z_move(own_block, p, 1).start()
 
-        if p < 3:
+        if p < X_CHUNKS:
             move(own_block, p, x_sem, x_dev).start()
 
     def arrived(o, p):
@@ -296,20 +298,20 @@
         def _():
             z_move(o, p, 1).start()
 
-        if p < 3:
+        if p < X_CHUNKS:
             move(o, p, x_sem, x_dev).start()
-        if p == 0:
+        if p < CHUNKS - Z_CHUNKS:
             move(o, p, y_sem, y_dev).start()
 
     def from_x(j, p):
         o = 2 * layer(j) + (1 - x)
         arrived(o, p)
-        if p < 2:
+        if p < CHUNKS - X_CHUNKS:
             move(o, p, y_sem, y_dev).start()
 
     def settle(q):
         here = tile_slice(q)
-        idx = index[here]
+        idx = index[q]
         spectrum = spectra[row_slice(q)]
         masks = []
         for t in range(per):
@@ -341,32 +343,46 @@
     spread[...] = jnp.full(spread.shape, -1, jnp.int32)
     spread[: listed.shape[0], : listed.shape[1]] = jnp.where(position < raw_count[...], listed, -1)
     spread[...] = jnp.transpose(jnp.concatenate([spread[: listed.shape[0]]] * 4, axis=0))
-    index[...] = jnp.where(
+    joined = jnp.where(
         second > 0, spread[pl.ds(1, tiles, stride=2)], spread[pl.ds(0, tiles, stride=2)]
     )
+    index[...] = jnp.full(index.shape, -1, jnp.int32)
+    kept[...] = jnp.zeros(kept.shape, jnp.float32)
+    for q in range(CHUNKS):
+        index[q, :per] = joined[q * per : (q + 1) * per]
     index_copy = remote(index, index_other, small_send.at[0], small_recv.at[0], y_dev)
     index_copy.start()
     for load in loads[2:5]:
         load.wait()
     forward(0)
-    forward(CHUNKS - 1)
+    token_local.start()
+    token_copy.start()
+    last = CHUNKS - 1
+    forward(last)
+    loads[5].wait()
     forward(1)
-    loads[5].wait()
+    forward(last - 1)
     index_copy.wait_recv()
     step(0)
+    forward(2)
+    forward(last - 2)
+    step(1)
     forward(3)
-    step(1)
+    forward(last - 3)
+    step(2)
     near(0)
     from_x(0, 0)
-    forward(2)
-    step(2)
+    forward(4)
+    forward(last - 4)
+    step(3)
     near(1)
     from_x(0, 1)
-    step(3)
-    near(2)
-    from_x(0, 2)
-    step(4)
-    near(3)
+    for p in range(2, Z_CHUNKS):
+        if p + 2 < Z_CHUNKS:
+            step(p + 2)
+        near(p)
+        if p < X_CHUNKS:
+            from_x(0, p)
 
     token_local.wait()
     token_copy.wait_recv()
@@ -380,7 +396,7 @@
         o = 2 * layer(j)
 
         def product(k):
-            deep = pl.ds(pl.multiple_of(k * rows, rows), rows)
+            deep = pl.ds(k * 2 * rows if isinstance(k, int) else pl.multiple_of(k * 2 * rows, 2 * rows), 2 * rows)
             both = jnp.concatenate([blocks[o, deep], blocks[o + 1, deep]], axis=1)
             return dot(tokens[:, deep], both)
 
@@ -390,22 +406,35 @@
             total[j] += product(k)
             return carry
 
-        lax.fori_loop(1, CHUNKS, add, 0)
+        lax.fori_loop(1, CHUNKS // 2, add, 0)
         part_copy(j).start()
 
-    for j in range(4):
+    def rest(j):
         if j > 0:
-            for p in range(4):
-                if j < 3:
-                    (far, farthest)[j - 1](p)
-                if p < 3:
-                    from_x(j, p)
-                if j < 3 and 4 * (j - 1) + p < CHUNKS:
-                    settle(4 * (j - 1) + p)
-            arrived(2 * layer(j) + x, 4)
-        arrived(2 * layer(j) + (1 - x), 4)
-        arrived(2 * layer(j) + (1 - x), 3)
+            for p in range(Z_CHUNKS, CHUNKS):
+                arrived(2 * layer(j) + x, p)
+        for p in range(X_CHUNKS, CHUNKS):
+            arrived(2 * layer(j) + (1 - x), p)
         multiply(j)
+
+    work = [functools.partial(step, p) for p in range(Z_CHUNKS, CHUNKS)]
+    work.append(functools.partial(rest, 0))
+    work += [functools.partial(settle, q) for q in range(5)]
+    work.append(functools.partial(rest, 1))
+    work += [functools.partial(settle, q) for q in range(5, CHUNKS)]
+    for arrival, j in ((far, 1), (farthest, 2)):
+        for p in range(Z_CHUNKS):
+            arrival(p)
+            if p < X_CHUNKS:
+                from_x(j, p)
+            if work:
+                work.pop(0)()
+    for one in work:
+        one()
+    rest(2)
+    for p in range(X_CHUNKS):
+        from_x(3, p)
+    rest(3)
 
     for j in range(4):
         part_copy(j).wait_recv()
@@ -423,7 +452,7 @@
         above = layer(j) > z
         goes_up = jnp.logical_and(jnp.logical_not(above), up_ok)
         goes_down = jnp.logical_and(jnp.logical_not(below), down_ok)
-        for p in range(4):
+        for p in range(Z_CHUNKS):
 
             @pl.when(goes_up)
             def _():
@@ -433,11 +462,12 @@
             def _():
                 z_move(o, p, 1).wait_send()
 
-            if p < 3:
+            if p < X_CHUNKS:
                 move(o, p, x_sem, x_dev).wait_send()
         if j > 0:
-            move(o, 0, y_sem, y_dev).wait_send()
-        for p in range(2):
+            for p in range(CHUNKS - Z_CHUNKS):
+                move(o, p, y_sem, y_dev).wait_send()
+        for p in range(CHUNKS - X_CHUNKS):
             move(2 * layer(j) + (1 - x), p, y_sem, y_dev).wait_send()
 
 
@@ -471,10 +501,10 @@
             pltpu.VMEM((4, 2 * own_tokens, 2 * cols), jnp.float32),
             pltpu.VMEM((4, own_tokens, 2 * cols), jnp.float32),
             pltpu.VMEM((half, cols), jnp.float32),
-            pltpu.VMEM((tiles, cols), jnp.float32),
-            pltpu.VMEM((tiles, cols), jnp.float32),
-            pltpu.VMEM((tiles, cols), jnp.int32),
-            pltpu.VMEM((tiles, cols), jnp.int32),
+            pltpu.VMEM((CHUNKS, 8, cols), jnp.float32),
+            pltpu.VMEM((CHUNKS, 8, cols), jnp.float32),
+            pltpu.VMEM((CHUNKS, 8, cols), jnp.int32),
+            pltpu.VMEM((CHUNKS, 8, cols), jnp.int32),
             pltpu.VMEM(weight.shape, weight.dtype),
             pltpu.VMEM(momentum.shape[1:], momentum.dtype),
             pltpu.VMEM(gradient.shape[1:], gradient.dtype),

time: 74.2 us -> 72.6 us (0.978)
  Pallas kernels: 69.2 us -> 67.7 us
    pallas_call x1, Pallas kernels: 69.2 us -> 67.7 us  [fused(): pl.pallas_call(fused_kernel, out_shape=(jax.ShapeDtypeStruct((own_tokens,...]
where the time goes in v4:
time: 72.6 us; the launch traced here: 72.3 us
  Pallas kernels  67.7 us (93%)
  local copies, waits for them, and re-layouts  3.95 us (5%)
    pallas_call x1, Pallas kernels, fused(): pl.pallas_call(fused_kernel, out_shape=(jax.ShapeDtypeStruct((own_tokens,...  67.7 us
    unnamed x9, local copies, waits for them, and re-layouts  3.95 us

profile of v4, /device:TPU:7, one launch (start us, length us, event | category | flops | bytes accessed | tf_op | source)
XLA Modules:
  0.0 72.3 jit_solution(640028414740665725)
XLA Ops:
  0.6 0.0 copy-start
  0.6 0.7 copy-done
  1.4 0.0 copy-start.1
  1.4 0.7 copy-done.1
  2.0 67.7 %shard_map.94 = (bf16[256,1024]{1,0:T(8,128)(2,1)S(1)}, bf16[40,32,128]{2,1,0:T(8,128)(2,1)S(1)}, f32[1,40,64,128]{3,2,1,0:T(8,128)}) custom-call(bf16[256,5120]{1,0:T(8,128)(2,1)} %hidden.1, bf16[40,64,128]{2,1,0:T(8,128)(2,1)} %weight_hbm.1, f32[1,40,64,128]{3,2,1,0:T(8,128)} %momentum_hbm.1, bf16[1,40,64,128]{3,2,1,0:T(8,128)(2,1)} %gradient_hbm.1, ...), custom_call_target="tpu_custom_call" | custom-call | tf_op jit(solution)/shard_map/pallas_call | solution.py:489
  69.8 0.0 copy-start.2
  69.8 0.8 %copy.13 = bf16[256,1024]{1,0:T(8,128)(2,1)} copy(bf16[256,1024]{1,0:T(8,128)(2,1)S(1)} %get-tuple-element.6) | data formatting | bytes 1048576
  70.6 0.7 %copy.14 = bf16[40,32,128]{2,1,0:T(8,128)(2,1)} copy(bf16[40,32,128]{2,1,0:T(8,128)(2,1)S(1)} %get-tuple-element.7) | data formatting | bytes 655360
  71.3 0.0 copy-done.2
  71.3 1.1 %copy.15 = f32[1,40,64,128]{3,2,1,0:T(8,128)} copy(f32[1,40,64,128]{3,2,1,0:T(8,128)S(1)} %copy-done.2) | data formatting | bytes 2621440
Async XLA Ops:
  0.6 0.7 copy-start
  1.4 0.7 copy-start.1
  69.8 1.5 %copy-start.2 = (f32[1,40,64,128]{3,2,1,0:T(8,128)S(1)}, f32[1,40,64,128]{3,2,1,0:T(8,128)}, u32[]{:S(2)}) copy-start(f32[1,40,64,128]{3,2,1,0:T(8,128)} %get-tuple-element.8) | copy-start | bytes 3932164

commit v5 on v4

--- a/solution.py
+++ b/solution.py
@@ -38,20 +38,12 @@
     return lax.dot_general(a, b, (((1,), (1,)), ((), ())), preferred_element_type=jnp.float32)
 
 
-def split3(value):
-    high = value.astype(jnp.bfloat16)
-    rest = value - high.astype(jnp.float32)
-    middle = rest.astype(jnp.bfloat16)
-    return high, middle, (rest - middle.astype(jnp.float32)).astype(jnp.bfloat16)
-
-
 def fused_kernel(
     hidden,
     weight_hbm,
     momentum_hbm,
     gradient_hbm,
     indices,
-    counts,
     basis_hbm,
     keys,
     update,
@@ -70,7 +62,6 @@
     gradient,
     basis,
     raw_index,
-    raw_count,
     spread,
     load_sem,
     recv_sem,
@@ -89,7 +80,6 @@
         for n, (src, dst) in enumerate(
             (
                 (indices.at[0], raw_index),
-                (counts, raw_count),
                 (basis_hbm, basis),
                 (momentum_hbm.at[0], momentum),
                 (gradient_hbm.at[0], gradient),
@@ -198,23 +188,14 @@
         right = [basis[n, :wide, :wide] for n in (0, 1)]
         part = dot(one, right[0]) + (dot(one, right[1]) + dot(two, right[0]))
         one, two = split(part)
-        return stacked(dot(basis[3], one) + (dot(basis[3], two) + dot(basis[4], one)))
+        return stacked(dot(basis[2], one) + (dot(basis[2], two) + dot(basis[3], one)))
 
     def transform(value):
-        one, two, three = split3(both_halves(value))
-        right = [basis[n, :wide, :wide] for n in (3, 4, 5)]
-        part = dot(one, right[0]) + (
-            (dot(one, right[1]) + dot(two, right[0]))
-            + (dot(one, right[2]) + dot(two, right[1]) + dot(three, right[0]))
-        )
-        one, two, three = split3(part)
-        return stacked(
-            dot(basis[0], one)
-            + (
-                (dot(basis[0], two) + dot(basis[1], one))
-                + (dot(basis[0], three) + dot(basis[1], two) + dot(basis[2], one))
-            )
-        )
+        one, two = split(both_halves(value))
+        right = [basis[n, :wide, :wide] for n in (2, 3)]
+        part = dot(one, right[0]) + (dot(one, right[1]) + dot(two, right[0]))
+        one, two = split(part)
+        return stacked(dot(basis[0], one) + (dot(basis[0], two) + dot(basis[1], one)))
 
     def tile_slice(q):
         return pl.ds(q * per if isinstance(q, int) else pl.multiple_of(q * per, per), per)
@@ -337,11 +318,9 @@
             from_z(layer(3), p)
 
     loads[0].wait()
-    loads[1].wait()
     listed = raw_index[...]
-    position = lax.broadcasted_iota(jnp.int32, listed.shape, 0)
     spread[...] = jnp.full(spread.shape, -1, jnp.int32)
-    spread[: listed.shape[0], : listed.shape[1]] = jnp.where(position < raw_count[...], listed, -1)
+    spread[: listed.shape[0], : listed.shape[1]] = listed
     spread[...] = jnp.transpose(jnp.concatenate([spread[: listed.shape[0]]] * 4, axis=0))
     joined = jnp.where(
         second > 0, spread[pl.ds(1, tiles, stride=2)], spread[pl.ds(0, tiles, stride=2)]
@@ -352,14 +331,14 @@
         index[q, :per] = joined[q * per : (q + 1) * per]
     index_copy = remote(index, index_other, small_send.at[0], small_recv.at[0], y_dev)
     index_copy.start()
-    for load in loads[2:5]:
+    for load in loads[1:4]:
         load.wait()
     forward(0)
     token_local.start()
     token_copy.start()
     last = CHUNKS - 1
     forward(last)
-    loads[5].wait()
+    loads[4].wait()
     forward(1)
     forward(last - 1)
     index_copy.wait_recv()
@@ -432,9 +411,29 @@
     for one in work:
         one()
     rest(2)
-    for p in range(X_CHUNKS):
+
+    def piece(p):
+        first = pl.multiple_of(jnp.minimum(place(p), place(p + 1)) * rows, 2 * rows)
+        deep = pl.ds(first, 2 * rows)
+        o = 2 * layer(3)
+        both = jnp.concatenate([blocks[o, deep], blocks[o + 1, deep]], axis=1)
+        return dot(tokens[:, deep], both)
+
+    for p in range(CHUNKS - X_CHUNKS):
         from_x(3, p)
-    rest(3)
+    total[3] = piece(0)
+    total[3] += piece(2)
+    for p in range(CHUNKS - X_CHUNKS, X_CHUNKS):
+        from_x(3, p)
+    total[3] += piece(4)
+    for p in range(Z_CHUNKS, CHUNKS):
+        arrived(2 * layer(3) + x, p)
+        arrived(2 * layer(3) + (1 - x), p)
+    total[3] += piece(8)
+    for p in range(X_CHUNKS, Z_CHUNKS):
+        arrived(2 * layer(3) + (1 - x), p)
+    total[3] += piece(6)
+    part_copy(3).start()
 
     for j in range(4):
         part_copy(j).wait_recv()
@@ -476,10 +475,12 @@
     kept_count = indices.shape[2]
     half = tiles * side
     own_tokens = hidden.shape[0]
+    live = jnp.arange(kept_count, dtype=jnp.int32)[None, :, None] < counts[:, None, :]
+    listed = jnp.where(live, jnp.swapaxes(indices, 1, 2), -1)
     table = np.kron(np.eye(4), cosine_table(side))
     parts = []
     for rest in (table, table.T):
-        for _ in range(3):
+        for _ in range(2):
             parts.append(rest.astype(jnp.bfloat16))
             rest = rest - parts[-1].astype(np.float64)
     basis = jnp.asarray(np.stack(parts))
@@ -493,7 +494,7 @@
             jax.ShapeDtypeStruct((tiles, side // 2, cols), jnp.bfloat16),
             jax.ShapeDtypeStruct(momentum.shape, jnp.float32),
         ),
-        in_specs=[pl.BlockSpec(memory_space=pltpu.HBM)] * 7,
+        in_specs=[pl.BlockSpec(memory_space=pltpu.HBM)] * 6,
         out_specs=(vmem, vmem, vmem),
         scratch_shapes=[
             pltpu.VMEM((8, half, cols), jnp.bfloat16),
@@ -510,9 +511,8 @@
             pltpu.VMEM(gradient.shape[1:], gradient.dtype),
             pltpu.VMEM(basis.shape, basis.dtype),
             pltpu.VMEM((kept_count, 2 * tiles), indices.dtype),
-            pltpu.VMEM(counts.shape, counts.dtype),
             pltpu.VMEM((cols, cols), jnp.int32),
-            dma((6,)),
+            dma((5,)),
             dma((number,)),
             dma((2, number)),
             dma((number,)),
@@ -532,8 +532,7 @@
         weight,
         momentum,
         gradient,
-        jnp.swapaxes(indices, 1, 2),
-        counts,
+        listed,
         basis,
     )
     return keys, update, new_momentum

time: 72.6 us -> 69.6 us (0.959); the launches traced: 72.3 us -> 68.3 us
  Pallas kernels: 67.7 us -> 64.3 us
  local copies, waits for them, and re-layouts: 3.95 us -> 2.58 us
  other arithmetic: 0 us -> 0.73 us
    pallas_call x1, Pallas kernels: 67.7 us -> 64.3 us  [fused(): pl.pallas_call(fused_kernel, out_shape=(jax.ShapeDtypeStruct((own_tokens,...]
    unnamed x9 -> x5, local copies, waits for them, and re-layouts: 3.95 us -> 2.58 us
where the time goes in v5:
time: 69.6 us; the launch traced here: 68.3 us
  Pallas kernels  64.3 us (92%)
  local copies, waits for them, and re-layouts  2.58 us (4%)
  other arithmetic  0.73 us (1%)
    pallas_call x1, Pallas kernels, fused(): pl.pallas_call(fused_kernel, out_shape=(jax.ShapeDtypeStruct((own_tokens,...  64.3 us
    unnamed x5, local copies, waits for them, and re-layouts  2.58 us

profile of v5, /device:TPU:7, one launch (start us, length us, event | category | flops | bytes accessed | tf_op | source)
XLA Modules:
  0.0 68.3 jit_solution(11294284445816021677)
XLA Ops:
  0.6 0.7 %bitcast_select_fusion.indices = s32[1,32,80]{2,1,0:T(8,128)S(1)} fusion(s32[1,80,32]{1,2,0:T(8,128)} %param.11, s32[80]{0:T(128)} %bitcast.3), kind=kLoop, calls=%fused_computation | loop fusion | flops 5120 | bytes 20800 | tf_op jit(solution)/shard_map/jit(_where)/select_n | solution.py:479
  1.4 64.3 %shard_map.94 = (bf16[256,1024]{1,0:T(8,128)(2,1)S(1)}, bf16[40,32,128]{2,1,0:T(8,128)(2,1)S(1)}, f32[1,40,64,128]{3,2,1,0:T(8,128)}) custom-call(bf16[256,5120]{1,0:T(8,128)(2,1)} %hidden.1, bf16[40,64,128]{2,1,0:T(8,128)(2,1)} %weight_hbm.1, f32[1,40,64,128]{3,2,1,0:T(8,128)} %momentum_hbm.1, bf16[1,40,64,128]{3,2,1,0:T(8,128)(2,1)} %gradient_hbm.1, ...), custom_call_target="tpu_custom_call" | custom-call | tf_op jit(solution)/shard_map/pallas_call | solution.py:490
  65.7 0.0 copy-start
  65.7 0.8 %copy.13 = bf16[256,1024]{1,0:T(8,128)(2,1)} copy(bf16[256,1024]{1,0:T(8,128)(2,1)S(1)} %get-tuple-element.6) | data formatting | bytes 1048576
  66.5 0.7 %copy.14 = bf16[40,32,128]{2,1,0:T(8,128)(2,1)} copy(bf16[40,32,128]{2,1,0:T(8,128)(2,1)S(1)} %get-tuple-element.7) | data formatting | bytes 655360
  67.2 0.0 copy-done
  67.2 1.1 %copy.15 = f32[1,40,64,128]{3,2,1,0:T(8,128)} copy(f32[1,40,64,128]{3,2,1,0:T(8,128)S(1)} %copy-done) | data formatting | bytes 2621440
Async XLA Ops:
  65.7 1.5 %copy-start = (f32[1,40,64,128]{3,2,1,0:T(8,128)S(1)}, f32[1,40,64,128]{3,2,1,0:T(8,128)}, u32[]{:S(2)}) copy-start(f32[1,40,64,128]{3,2,1,0:T(8,128)} %get-tuple-element.8) | copy-start | bytes 3932164

commit v6 on v5

--- a/solution.py
+++ b/solution.py
@@ -14,7 +14,7 @@
 exact = lax.Precision.HIGHEST
 MESH = pl.DeviceIdType.MESH
 CHUNKS = 10
-Z_CHUNKS = 8
+Z_CHUNKS = 7
 X_CHUNKS = 6
 
 

time: 69.6 us -> 63 us (0.905); the launches traced: 68.3 us -> 62.7 us
  Pallas kernels: 64.3 us -> 58.8 us
    pallas_call x1, Pallas kernels: 64.3 us -> 58.8 us  [fused(): pl.pallas_call(fused_kernel, out_shape=(jax.ShapeDtypeStruct((own_tokens,...]
where the time goes in v6:
time: 63 us; the launch traced here: 62.7 us
  Pallas kernels  58.8 us (93%)
  local copies, waits for them, and re-layouts  2.58 us (4%)
  other arithmetic  0.73 us (1%)
  between operations  0.65 us (1%)
    pallas_call x1, Pallas kernels, fused(): pl.pallas_call(fused_kernel, out_shape=(jax.ShapeDtypeStruct((own_tokens,...  58.8 us
    unnamed x5, local copies, waits for them, and re-layouts  2.58 us

profile of v6, /device:TPU:7, one launch (start us, length us, event | category | flops | bytes accessed | tf_op | source)
XLA Modules:
  0.0 62.7 jit_solution(10232044557731079932)
XLA Ops:
  0.6 0.7 %bitcast_select_fusion.indices = s32[1,32,80]{2,1,0:T(8,128)S(1)} fusion(s32[1,80,32]{1,2,0:T(8,128)} %param.11, s32[80]{0:T(128)} %bitcast.3), kind=kLoop, calls=%fused_computation | loop fusion | flops 5120 | bytes 20800 | tf_op jit(solution)/shard_map/jit(_where)/select_n | solution.py:479
  1.4 58.8 %shard_map.94 = (bf16[256,1024]{1,0:T(8,128)(2,1)S(1)}, bf16[40,32,128]{2,1,0:T(8,128)(2,1)S(1)}, f32[1,40,64,128]{3,2,1,0:T(8,128)}) custom-call(bf16[256,5120]{1,0:T(8,128)(2,1)} %hidden.1, bf16[40,64,128]{2,1,0:T(8,128)(2,1)} %weight_hbm.1, f32[1,40,64,128]{3,2,1,0:T(8,128)} %momentum_hbm.1, bf16[1,40,64,128]{3,2,1,0:T(8,128)(2,1)} %gradient_hbm.1, ...), custom_call_target="tpu_custom_call" | custom-call | tf_op jit(solution)/shard_map/pallas_call | solution.py:490
  60.1 0.0 copy-start
  60.1 0.8 %copy.13 = bf16[256,1024]{1,0:T(8,128)(2,1)} copy(bf16[256,1024]{1,0:T(8,128)(2,1)S(1)} %get-tuple-element.6) | data formatting | bytes 1048576
  60.9 0.7 %copy.14 = bf16[40,32,128]{2,1,0:T(8,128)(2,1)} copy(bf16[40,32,128]{2,1,0:T(8,128)(2,1)S(1)} %get-tuple-element.7) | data formatting | bytes 655360
  61.7 0.0 copy-done
  61.7 1.1 %copy.15 = f32[1,40,64,128]{3,2,1,0:T(8,128)} copy(f32[1,40,64,128]{3,2,1,0:T(8,128)S(1)} %copy-done) | data formatting | bytes 2621440
Async XLA Ops:
  60.1 1.5 %copy-start = (f32[1,40,64,128]{3,2,1,0:T(8,128)S(1)}, f32[1,40,64,128]{3,2,1,0:T(8,128)}, u32[]{:S(2)}) copy-start(f32[1,40,64,128]{3,2,1,0:T(8,128)} %get-tuple-element.8) | copy-start | bytes 3932164
